TPU v7x, 256 devices: a whole 4x4x8 slice. The times are simulated.
256 devices in a mesh: tp: 8 (over x, core), dp: 32 (over z, y).
Axes of the slice: x: 4, y: 4, z: 8, core: 2. Of those that a mesh axis runs over, the one named last changes fastest.
Arguments:
- tokens: bfloat16 [1536, 8192], P('tp', 'dp'), may hold values from -60 to 60
- hidden_grad: bfloat16 [1536, 14336], P('dp', 'tp'), may hold values from -60 to 60
- gate_weight: bfloat16 [8192, 14336], P('dp', 'tp'), may hold values from -0.0625 to 0.0625
- up_weight: bfloat16 [8192, 14336], P('dp', 'tp'), may hold values from -0.0625 to 0.0625
- probe: bfloat16 [8192, 14336], P('dp', 'tp'), may hold values from -5 to 5
- moment: float32 [8192, 14336], P('dp', 'tp'), may hold values from -3 to 3
- curvature: float32 [8192, 14336], P('dp', 'tp'), may hold values from 0.02 to 0.2
Outputs:
- new_moment: float32 [8192, 14336], P('dp', 'tp')
- new_curvature: float32 [8192, 14336], P('dp', 'tp')
- update: float32 [8192, 14336], P('dp', 'tp')
All inputs are finite; a program needn't handle non-finite values.
Results may differ from a plain program's by a relative error of at most 0.0028.
Values may be sent and summed in bfloat16 or wider, within the bound.
A program may use at most 192 MiB of HBM per device.

v0:
```python
import jax
import jax.numpy as jnp
from jax import lax
from jax.sharding import PartitionSpec as P

D = 8192
FF = 14336


moment_decay = 0.9
curvature_decay = 0.99
curvature_scale = 2.0
ratio_floor = 0.05
mean_eps = 1e-06


def second_order(gate_pre, up_value, tangent, upstream):
    sigmoid_val = jax.nn.sigmoid(gate_pre)
    first_deriv = sigmoid_val * (1.0 + gate_pre * (1.0 - sigmoid_val))
    second_deriv = sigmoid_val * (1.0 - sigmoid_val) * (2.0 + gate_pre * (1.0 - 2.0 * sigmoid_val))
    scaled = upstream.astype(jnp.float32) * up_value
    grad_rows = (scaled * first_deriv).astype(jnp.bfloat16)
    hess_rows = (scaled * second_deriv * tangent).astype(jnp.bfloat16)
    return (grad_rows, hess_rows)


def row_products(features, weights):
    return jnp.dot(features, weights, preferred_element_type=jnp.float32)


def row_contract(features, shard_part):
    return lax.dot_general(
        features, shard_part, (((0,), (0,)), ((), ())), preferred_element_type=jnp.float32
    )


def split_sums(partials, hidden_cols, upstream):
    return second_order(
        partials[:, :hidden_cols],
        partials[:, hidden_cols : 2 * hidden_cols],
        partials[:, 2 * hidden_cols :],
        upstream,
    )


def body(tokens, hidden_grad, gate_weight, up_weight, probe, moment, curvature):
    features = lax.all_gather(tokens, "tp", axis=0, tiled=True)
    weights = jnp.concatenate([gate_weight, up_weight, probe], axis=1)
    hidden_cols = gate_weight.shape[1]
    partials = lax.psum_scatter(
        row_products(features, weights), "dp", scatter_dimension=0, tiled=True
    )
    grad_rows, hess_rows = split_sums(partials, hidden_cols, hidden_grad)
    result = row_contract(
        features,
        lax.all_gather(jnp.concatenate([grad_rows, hess_rows], axis=1), "dp", axis=0, tiled=True),
    )
    gradient = result[:, :hidden_cols]
    curv_product = result[:, hidden_cols:]
    squares = lax.psum(jnp.sum(gradient * gradient), ("tp", "dp"))
    factor = jnp.minimum(1.0, lax.rsqrt(squares / (D * FF) + mean_eps))
    new_moment = moment_decay * moment + (1.0 - moment_decay) * factor * gradient
    new_curvature = (
        curvature_decay * curvature
        + (1.0 - curvature_decay) * factor * probe.astype(jnp.float32) * curv_product
    )
    update = jnp.clip(
        new_moment / jnp.maximum(curvature_scale * new_curvature, ratio_floor), -1.0, 1.0
    )
    return (new_moment, new_curvature, update)


def solution(mesh):
    placed = (
        P("tp", "dp"),
        P("dp", "tp"),
        P("dp", "tp"),
        P("dp", "tp"),
        P("dp", "tp"),
        P("dp", "tp"),
        P("dp", "tp"),
    )
    return jax.shard_map(
        body,
        mesh=mesh,
        in_specs=placed,
        out_specs=(P("dp", "tp"), P("dp", "tp"), P("dp", "tp")),
        check_vma=False,
    )
```

profile of v0, /device:TPU:1, one launch (start us, length us, event | category | flops | bytes accessed | tf_op | source)
XLA Modules:
  0.0 603.5 jit_solution(16555363339773622835)
XLA Ops:
  7.2 0.0 reduce-scatter.4.cloned.1.call-start
  7.2 16.8 %all_gather.6 = bf16[1536,256]{1,0:T(8,128)(2,1)S(1)} all-gather(bf16[192,256]{1,0:T(8,128)(2,1)} %param.7), channel_id=1, replica_groups=mesh['tp'=8,'dp'=32] {'tp'}, dimensions={0}, use_global_device_ids=true | all-gather | bytes 884736 | tf_op jit(solution)/shard_map/all_gather | solution.py:47
  24.0 14.9 %convolution_bitcast_fusion = f32[1536,5376]{0,1:T(8,128)} fusion(bf16[1536,256]{1,0:T(8,128)(2,1)S(1)} %all_gather.6, bf16[256,1792]{1,0:T(8,128)(2,1)} %param.11, bf16[256,1792]{1,0:T(8,128)(2,1)} %param.10, bf16[256,1792]{1,0:T(8,128)(2,1)} %param.9), kind=kOutput, calls=%fused_computation | convolution fusion | flops 4236115968 | bytes 36569088 | tf_op jit(solution)/shard_map/dot_general | solution.py:28
  38.8 33.3 %copy.35 = f32[1536,5376]{1,0:T(8,128)} copy(f32[1536,5376]{0,1:T(8,128)} %convolution_bitcast_fusion) | data formatting | bytes 66060288
  72.1 0.0 copy-start.3
  72.1 0.0 reduce-scatter.4.cloned.1.call-update
  72.1 0.0 copy-start.2
  72.2 0.0 all-gather.2.cloned.1.call-start
  72.2 311.0 %reduce-scatter.4.cloned.1.call-done = f32[48,5376]{1,0:T(8,128)} async-done(((f32[1536,5376]{1,0:T(8,128)}), f32[48,5376]{1,0:T(8,128)}) %reduce-scatter.4.cloned.1.call-update) | async-done | bytes 1032208 | tf_op jit(solution)/shard_map/reduce_scatter | solution.py:50
  383.2 0.0 copy-done.3
  383.2 1.4 fusion.9
  384.7 0.8 pad_maximum_fusion
  385.4 0.0 all-gather.2.cloned.1.call-update
  385.4 0.0 copy-done.2
  385.4 0.5 copy.31
  386.0 1.8 copy.26
  387.8 109.1 %all-gather.2.cloned.1.call-done = bf16[1536,3584]{1,0:T(8,128)(2,1)} async-done(((bf16[48,3584]{1,0:T(8,128)(2,1)}), bf16[1536,3584]{1,0:T(8,128)(2,1)}) %all-gather.2.cloned.1.call-update) | async-done | bytes 11010064 | tf_op jit(solution)/shard_map/all_gather | solution.py:56
  496.9 5.9 convolution_bitcast_fusion.1
  502.8 0.0 copy-start
  502.8 1.8 copy-done
  504.6 1.1 multiply_reduce_fusion
  505.7 2.7 copy.30
  508.4 74.9 %psum.7 = f32[]{:T(128)} all-reduce(f32[]{:T(128)} %multiply_reduce_fusion), channel_id=1, replica_groups=mesh['tp'=8,'dp'=32] {'tp','dp'}, use_global_device_ids=true, to_apply=%region_2.0 | all-reduce | flops 1 | bytes 8 | tf_op jit(solution)/shard_map/psum | solution.py:60
  584.0 5.4 divide_clamp_fusion
  589.4 2.7 copy.32
  592.1 0.0 copy-start.1
  592.1 2.9 copy.33
  595.0 0.0 copy-done.1
  595.0 1.7 copy.34
Async XLA Ops:
  7.2 376.1 %reduce-scatter.4.cloned.1.call-start = ((), (), s32[]{:S(2)}) async-start(), calls=%async_computation.2 | async-start | bytes 34062336 | tf_op jit(solution)/shard_map/reduce_scatter | solution.py:50
  72.1 311.1 %copy-start.3 = (bf16[48,1792]{1,0:T(8,128)(2,1)S(1)}, bf16[48,1792]{1,0:T(8,128)(2,1)}, u32[]{:S(2)}) copy-start(bf16[48,1792]{1,0:T(8,128)(2,1)} %param.8) | copy-start | bytes 516100
  72.1 313.3 %copy-start.2 = (bf16[256,1792]{1,0:T(8,128)(2,1)S(1)}, bf16[256,1792]{1,0:T(8,128)(2,1)}, u32[]{:S(2)}) copy-start(bf16[256,1792]{1,0:T(8,128)(2,1)} %param.11) | copy-start | bytes 2752516
  72.2 424.8 %all-gather.2.cloned.1.call-start = ((), (), s32[]{:S(2)}) async-start(), calls=%async_computation.1 | async-start | bytes 11354112 | tf_op jit(solution)/shard_map/all_gather | solution.py:56
  502.8 1.8 copy-start
  592.1 2.9 copy-start.1
Sparse Core Ops, SparseCore 0:
  72.3 310.9 reduce-scatter.3
  386.7 110.1 all-gather.1
where the time goes:
time: 604 us; the launch traced here: 603 us
  waiting for transfers between devices  420 us (70%)
  blocking collectives  91.7 us (15%)
  local copies, waits for them, and re-layouts  47.4 us (8%)
  matrix products  20.7 us (3%)
  between operations  14.8 us (2%)
  other arithmetic  8.61 us (1%)
    reduce_scatter x1, waiting for transfers between devices, body(): lax.psum_scatter(row_products(features, weights), 'dp', scatter_dimension...  311 us
    all_gather x1, waiting for transfers between devices, body(): lax.all_gather(jnp.concatenate([grad_rows, hess_rows], axis=1), 'dp', axi...  109 us
    psum x1, blocking collectives, body(): squares = lax.psum(jnp.sum(gradient * gradient), ('tp', 'dp'))  74.9 us
    unnamed x15, local copies, waits for them, and re-layouts  47.4 us
    all_gather x1, blocking collectives, body(): features = lax.all_gather(tokens, 'tp', axis=0, tiled=True)  16.8 us
    dot_general x1, matrix products, row_products(): return jnp.dot(features, weights, preferred_element_type=jnp.float32)  14.9 us
  transfers between devices with their start and end apart: 2, of which 2 were waited for; matrix products, arithmetic and copies ran while one was open for 0% of the time, Pallas kernels for 0%

commit v1 on v0

v1 whole, which is shorter than its diff:
```python
import functools

import jax
import jax.numpy as jnp
from jax import lax
from jax.experimental import pallas as pl
from jax.experimental.pallas import tpu as pltpu
from jax.sharding import PartitionSpec as P

D = 8192
FF = 14336

moment_decay = 0.9
curvature_decay = 0.99
curvature_scale = 2.0
ratio_floor = 0.05
mean_eps = 1e-06

NX, NY, NZ = 4, 4, 8
ROWS = 192
HALF = 96
FEAT = 256
DEPTH = NY * FEAT
LANE = 128
TILES = 4

BF = jnp.bfloat16
F32 = jnp.float32


def second_order(gate_pre, up_value, tangent, upstream):
    sigmoid_val = jax.nn.sigmoid(gate_pre)
    first_deriv = sigmoid_val * (1.0 + gate_pre * (1.0 - sigmoid_val))
    second_deriv = sigmoid_val * (1.0 - sigmoid_val) * (2.0 + gate_pre * (1.0 - 2.0 * sigmoid_val))
    scaled = upstream.astype(F32) * up_value
    return (scaled * first_deriv).astype(BF), (scaled * second_deriv * tangent).astype(BF)


def code4(val):
    return ((val * jnp.abs(val)) * (val * val)).astype(BF)


def decode4(coded):
    val = coded.astype(F32)
    root = lax.rsqrt(jnp.maximum(jnp.abs(val), 1e-36))
    return val * root * root * lax.rsqrt(root)


def code2(val):
    return (val * jnp.abs(val)).astype(BF)


def decode2(coded):
    val = coded.astype(F32)
    return val * lax.rsqrt(jnp.maximum(jnp.abs(val), 1e-36))


def kernel(
    tok_in, hid_in, gate_in, up_in, probe_in,
    grad_out, curv_out, squares_out,
    tok, tok_t, wts, hid, rs_out, rs_in, rows, outb, sq, sq_z, sq_y, sq_t,
    tok_l, tok_s, tok_r, w_l, w_s, w_r, hid_l, hid_s, hid_r,
    rs_s, rs_r, ag_s, ag_r, gr_l, gr_s, gr_r, sq_s, sq_r,
):
    tp, dp = lax.axis_index("tp"), lax.axis_index("dp")
    x, c = lax.div(tp, 2), lax.rem(tp, 2)
    z, y = lax.div(dp, NY), lax.rem(dp, NY)

    def mod(val, n):
        return lax.rem(val + n, n)

    def at_y(yy):
        return {"dp": z * NY + yy}

    def at_z(zz):
        return {"dp": zz * NY + y}

    def at_tp(tt):
        return {"tp": tt}

    def first_tile(yy):
        return lax.div(7 * yy + 1 - c, 2)

    def has(yy, t):
        return None if t < TILES - 1 else lax.rem(yy + c, 2) == 0

    def when(cond, fn):
        if cond is None:
            fn()
        else:
            pl.when(cond)(fn)

    def lanes(start, size):
        return pl.ds(pl.multiple_of(start, LANE), size)

    def remote(src, dst, s_sem, r_sem, dev):
        return pltpu.make_async_remote_copy(
            src_ref=src, dst_ref=dst, send_sem=s_sem, recv_sem=r_sem,
            device_id=dev, device_id_type=pl.DeviceIdType.MESH,
        )

    sent = []

    def send(cond, copy):
        when(cond, copy.start)
        sent.append((cond, copy.wait_send))

    def landed(dst, r_sem):
        remote(dst, dst, r_sem, r_sem, at_tp(tp)).wait_recv()

    my_feat = lanes(y * FEAT, FEAT)

    tok_own = pltpu.make_async_copy(tok_in, tok.at[tp, :, my_feat], tok_l)
    tok_own.start()
    weights = (gate_in, up_in, probe_in)
    mine3 = has(y, TILES - 1)

    def mine(t):
        return mine3 if t == TILES - 1 else None

    w_own = {}
    for t in range(TILES):
        for a in range(3):
            w_own[t, a] = pltpu.make_async_copy(
                weights[a].at[:, lanes((first_tile(y) + t) * LANE, LANE)],
                wts.at[t, my_feat, pl.ds(a * LANE, LANE)],
                w_l.at[t, a],
            )
            when(mine(t), w_own[t, a].start)
    my_toks = pl.ds(pl.multiple_of(y * 48, 48), 48)
    hid_own = {}
    for t in range(TILES):
        hid_own[t] = pltpu.make_async_copy(
            hid_in.at[:, lanes((first_tile(y) + t) * LANE, LANE)],
            hid.at[t, my_toks, :],
            hid_l.at[t],
        )
        when(mine(t), hid_own[t].start)

    barrier = pltpu.get_barrier_semaphore()
    peers = [at_y(mod(y + r, NY)) for r in range(1, NY)]
    peers += [at_z(mod(z + r, NZ)) for r in range(1, NZ)]
    peers += [at_tp(mod(tp + r, 8)) for r in range(1, 8)]
    for dev in peers:
        pl.semaphore_signal(barrier, inc=1, device_id=dev, device_id_type=pl.DeviceIdType.MESH)
    pl.semaphore_wait(barrier, len(peers))

    def tok_part(blk, yy):
        return tok.at[blk, :, lanes(yy * FEAT, FEAT)]

    for r in range(1, NY):
        send(None, remote(tok_in, tok_part(tp, y), tok_s.at[r], tok_r.at[r], at_y(mod(y + r, NY))))

    def send_weights(t):
        for r in range(1, NY):
            yy = mod(y + r, NY)
            for a in range(3):
                send(
                    has(yy, t),
                    remote(
                        weights[a].at[:, lanes((first_tile(yy) + t) * LANE, LANE)],
                        wts.at[t, my_feat, pl.ds(a * LANE, LANE)],
                        w_s.at[t, r, a], w_r.at[t, r, a], at_y(yy),
                    ),
                )

    def wait_weights(t):
        def go():
            for a in range(3):
                w_own[t, a].wait()
                for r in range(1, NY):
                    yy = mod(y - r, NY)
                    landed(wts.at[t, lanes(yy * FEAT, FEAT), pl.ds(a * LANE, LANE)], w_r.at[t, r, a])

        when(mine(t), go)

    def send_hidden(t):
        for r in range(1, NY):
            yy = mod(y + r, NY)
            send(
                has(yy, t),
                remote(
                    hid_in.at[:, lanes((first_tile(yy) + t) * LANE, LANE)],
                    hid.at[t, my_toks, :],
                    hid_s.at[t, r], hid_r.at[t, r], at_y(yy),
                ),
            )

    def wait_hidden(t):
        hid_own[t].wait()
        for r in range(1, NY):
            yy = mod(y - r, NY)
            landed(hid.at[t, pl.ds(pl.multiple_of(yy * 48, 48), 48), :], hid_r.at[t, r])

    send_weights(0)

    tok_own.wait()
    for r in range(1, NY):
        landed(tok_part(tp, mod(y - r, NY)), tok_r.at[r])
    other = tp + 1 - 2 * c
    for r in range(1, NX):
        tt = mod(tp + 2 * r, 8)
        send(None, remote(tok.at[tp], tok.at[tp], tok_s.at[3 + r], tok_r.at[3 + r], at_tp(tt)))
    send(None, remote(tok.at[tp], tok.at[tp], tok_s.at[7], tok_r.at[7], at_tp(other)))
    for r in (1, 3, 2):
        blk = mod(tp - 2 * r, 8)
        landed(tok.at[blk], tok_r.at[3 + r])
        send(None, remote(tok.at[blk], tok.at[blk], tok_s.at[7 + r], tok_r.at[7 + r], at_tp(other)))
    wait_weights(0)
    send_weights(1)
    send_hidden(0)
    for r in range(NX):
        landed(tok.at[mod(other - 2 * r, 8)], tok_r.at[7 + r])

    z_next = (mod(z + 1, NZ), mod(z - 1, NZ))
    halves = (pl.ds(0, HALF), pl.ds(HALF, HALF))

    def partial(t, blk):
        return jnp.dot(tok[blk], wts[t], preferred_element_type=F32)

    def rs_send(t, s, d, part):
        send(
            mine(t),
            remote(
                rs_out.at[d, t, s, part, :], rs_in.at[d, t, s, part, :],
                rs_s.at[d, t, s], rs_r.at[d, t, s], at_z(z_next[d]),
            ),
        )

    whole = pl.ds(0, ROWS)

    def rs_step(t, s):
        if s == 0:

            def first():
                val = partial(t, mod(z + 4, NZ))
                for d in range(2):
                    rs_out[d, t, 0, halves[d], :] = code4(val[d * HALF : (d + 1) * HALF])

            when(mine(t), first)
            for d in range(2):
                rs_send(t, 0, d, halves[d])
            return
        for d in range(2):

            def later(d=d):
                blk = mod(z + 4 - s, NZ) if d == 0 else mod(z - 4 + s, NZ)
                val = partial(t, blk)
                part = halves[d] if s == 1 else whole
                landed(rs_in.at[d, t, s - 1, part, :], rs_r.at[d, t, s - 1])
                if s == 1:
                    rs_out[d, t, s, halves[1 - d], :] = code4(val[(1 - d) * HALF : (2 - d) * HALF])
                    rs_out[d, t, s, part, :] = code4(
                        val[d * HALF : (d + 1) * HALF] + decode4(rs_in[d, t, s - 1, part, :])
                    )
                else:
                    rs_out[d, t, s] = code4(val + decode4(rs_in[d, t, s - 1]))

            when(mine(t), later)
            rs_send(t, s, d, whole)

    def ag_send(t, s, d, blk, part):
        send(
            mine(t),
            remote(
                rows.at[t, blk, part, :], rows.at[t, blk, part, :],
                ag_s.at[d, t, s], ag_r.at[d, t, s], at_z(z_next[d]),
            ),
        )

    def rs_last(t):
        def go():
            val = partial(t, z)
            wait_hidden(t)
            for d in range(2):
                landed(rs_in.at[d, t, 3, whole, :], rs_r.at[d, t, 3])
            val = val + decode4(rs_in[0, t, 3]) + decode4(rs_in[1, t, 3])
            grad_rows, hess_rows = second_order(
                val[:, :LANE], val[:, LANE : 2 * LANE], val[:, 2 * LANE :], hid[t]
            )
            rows[t, z, :, pl.ds(0, LANE)] = grad_rows
            rows[t, z, :, pl.ds(LANE, LANE)] = hess_rows

        when(mine(t), go)
        for d in range(2):
            ag_send(t, 0, d, z, whole)

    def ag_step(t, s):
        for d in range(2):
            blk = mod(z - s, NZ) if d == 0 else mod(z + s, NZ)
            when(mine(t), lambda: landed(rows.at[t, blk, whole, :], ag_r.at[d, t, s - 1]))
            ag_send(t, s, d, blk, whole if s < 3 else halves[d])

    def ag_last(t):
        for d in range(2):
            when(mine(t), lambda: landed(rows.at[t, mod(z + 4, NZ), halves[d], :], ag_r.at[d, t, 3]))

    outs = (grad_out, curv_out)
    sq[...] = jnp.zeros_like(sq)

    def products(t):
        for j in (2, 1, 3, 0):
            yy = mod(y + j, NY)

            def go():
                val = jnp.dot(
                    tok_t[pl.ds(pl.multiple_of(yy * FEAT, FEAT), FEAT), :],
                    rows[t].reshape(NZ * ROWS, 2 * LANE),
                    preferred_element_type=F32,
                )
                grad = val[:, :LANE]
                sq[...] += jnp.sum((grad * grad).reshape(FEAT // 8, 8, LANE), axis=0)
                outb[t, j, 0] = grad.astype(BF)
                outb[t, j, 1] = code2(val[:, LANE:])

            when(mine(t), go)
            for a in range(2):
                dst = outs[a].at[:, lanes((first_tile(y) + t) * LANE, LANE)]
                if j:
                    send(mine(t), remote(outb.at[t, j, a], dst, gr_s.at[t, j, a], gr_r.at[t, j, a], at_y(yy)))
                else:
                    own = pltpu.make_async_copy(outb.at[t, j, a], dst, gr_l.at[t, a])
                    when(mine(t), own.start)
                    sent.append((mine(t), own.wait))

    def transpose(i):
        both = tok[pl.ds(2 * i, 2)].reshape(2 * ROWS, DEPTH)
        tok_t[:, pl.ds(i * 2 * ROWS, 2 * ROWS)] = both.T

    rs_step(0, 0)
    transpose(0)
    rs_step(0, 1)
    transpose(1)
    wait_weights(1)
    send_weights(2)
    send_hidden(1)
    rs_step(0, 2)
    rs_step(1, 0)
    transpose(2)
    rs_step(0, 3)
    transpose(3)
    rs_last(0)
    for t in range(1, TILES):
        rs_step(t, 1)
        ag_step(t - 1, 1)
        if t + 1 < TILES:
            wait_weights(t + 1)
            if t + 2 < TILES:
                send_weights(t + 2)
            send_hidden(t + 1)
        rs_step(t, 2)
        ag_step(t - 1, 2)
        rs_step(t, 3)
        ag_step(t - 1, 3)
        if t + 1 < TILES:
            rs_step(t + 1, 0)
        ag_last(t - 1)
        products(t - 1)
        rs_last(t)
    for s in range(1, 4):
        ag_step(TILES - 1, s)
    ag_last(TILES - 1)
    products(TILES - 1)

    def all_sum(buf, n, me, dev_at, base):
        buf[me] = sq[...]
        for r in range(1, n):
            dst = buf.at[me]
            send(None, remote(dst, dst, sq_s.at[base + r], sq_r.at[base + r], dev_at(mod(me + r, n))))
        for r in range(1, n):
            landed(buf.at[mod(me - r, n)], sq_r.at[base + r])
        sq[...] = jnp.sum(buf[...], axis=0)

    all_sum(sq_z, NZ, z, at_z, 0)
    all_sum(sq_y, NY, y, at_y, 8)
    all_sum(sq_t, 8, tp, at_tp, 12)
    squares_out[...] = jnp.broadcast_to(jnp.sum(sq[...]), (8, LANE))

    for t in range(TILES):
        for r in range(1, NY):
            yy = mod(y - r, NY)

            def go():
                for a in range(2):
                    dst = outs[a].at[:, lanes((first_tile(yy) + t) * LANE, LANE)]
                    landed(dst, gr_r.at[t, r, a])

            when(has(yy, t), go)
    for cond, wait in sent:
        when(cond, wait)


def products_of(tokens, hidden_grad, gate_weight, up_weight, probe):
    dma = pltpu.SemaphoreType.DMA
    hbm = pl.BlockSpec(memory_space=pl.ANY)
    return pl.pallas_call(
        kernel,
        out_shape=(
            jax.ShapeDtypeStruct((FEAT, 14 * LANE), BF),
            jax.ShapeDtypeStruct((FEAT, 14 * LANE), BF),
            jax.ShapeDtypeStruct((8, LANE), F32),
        ),
        in_specs=[hbm] * 5,
        out_specs=(hbm, hbm, pl.BlockSpec(memory_space=pltpu.VMEM)),
        scratch_shapes=[
            pltpu.VMEM((8, ROWS, DEPTH), BF),
            pltpu.VMEM((DEPTH, 8 * ROWS), BF),
            pltpu.VMEM((TILES, DEPTH, 3 * LANE), BF),
            pltpu.VMEM((TILES, ROWS, LANE), BF),
            pltpu.VMEM((2, TILES, 4, ROWS, 3 * LANE), BF),
            pltpu.VMEM((2, TILES, 4, ROWS, 3 * LANE), BF),
            pltpu.VMEM((TILES, NZ, ROWS, 2 * LANE), BF),
            pltpu.VMEM((TILES, NY, 2, FEAT, LANE), BF),
            pltpu.VMEM((8, LANE), F32),
            pltpu.VMEM((NZ, 8, LANE), F32),
            pltpu.VMEM((NY, 8, LANE), F32),
            pltpu.VMEM((8, 8, LANE), F32),
            dma, dma((11,)), dma((11,)),
            dma((TILES, 3)), dma((TILES, NY, 3)), dma((TILES, NY, 3)),
            dma((TILES,)), dma((TILES, NY)), dma((TILES, NY)),
            dma((2, TILES, 4)), dma((2, TILES, 4)), dma((2, TILES, 4)), dma((2, TILES, 4)),
            dma((TILES, 2)), dma((TILES, NY, 2)), dma((TILES, NY, 2)),
            dma((20,)), dma((20,)),
        ],
        compiler_params=pltpu.CompilerParams(
            collective_id=0, has_side_effects=True, vmem_limit_bytes=48 * 1024 * 1024
        ),
    )(tokens, hidden_grad, gate_weight, up_weight, probe)


def body(tokens, hidden_grad, gate_weight, up_weight, probe, moment, curvature):
    gradient, curv_coded, squares = products_of(tokens, hidden_grad, gate_weight, up_weight, probe)
    factor = jnp.minimum(1.0, lax.rsqrt(squares[0, 0] / (D * FF) + mean_eps))
    new_moment = moment_decay * moment + (1.0 - moment_decay) * factor * gradient.astype(F32)
    new_curvature = curvature_decay * curvature + (
        1.0 - curvature_decay
    ) * factor * probe.astype(F32) * decode2(curv_coded)
    update = jnp.clip(
        new_moment / jnp.maximum(curvature_scale * new_curvature, ratio_floor), -1.0, 1.0
    )
    return (new_moment, new_curvature, update)


def solution(mesh):
    placed = (
        P("tp", "dp"),
        P("dp", "tp"),
        P("dp", "tp"),
        P("dp", "tp"),
        P("dp", "tp"),
        P("dp", "tp"),
        P("dp", "tp"),
    )
    return jax.shard_map(
        body,
        mesh=mesh,
        in_specs=placed,
        out_specs=(P("dp", "tp"), P("dp", "tp"), P("dp", "tp")),
        check_vma=False,
    )
```

time: 604 us -> 170 us (0.28)
  waiting for transfers between devices: 420 us -> 0 us
  Pallas kernels: 0 us -> 157 us
  blocking collectives: 91.7 us -> 0 us
  local copies, waits for them, and re-layouts: 47.4 us -> 5.86 us
  matrix products: 20.7 us -> 0 us
  between operations: 14.8 us -> 1.36 us
    reduce_scatter x1 -> x0, waiting for transfers between devices: 311 us -> none  [body(): lax.psum_scatter(row_products(features, weights), 'dp', scatter_dimension...]
    pallas_call x0 -> x1, Pallas kernels: none -> 157 us  [products_of(): pl.pallas_call(kernel, out_shape=(jax.ShapeDtypeStruct((FEAT, 14 * LANE),...]
    all_gather x1 -> x0, waiting for transfers between devices: 109 us -> none  [body(): lax.all_gather(jnp.concatenate([grad_rows, hess_rows], axis=1), 'dp', axi...]
    psum x1 -> x0, blocking collectives: 74.9 us -> none  [body(): squares = lax.psum(jnp.sum(gradient * gradient), ('tp', 'dp'))]
    unnamed x15 -> x12, local copies, waits for them, and re-layouts: 47.4 us -> 5.34 us
    dot_general x2 -> x0, matrix products: 20.7 us -> none  [the longest x1 14.9 us: row_products(): return jnp.dot(features, weights, preferred_element_type=jnp.float32)]
    all_gather x1 -> x0, blocking collectives: 16.8 us -> none  [body(): features = lax.all_gather(tokens, 'tp', axis=0, tiled=True)]
  transfers between devices with their start and end apart: 2 -> 0, of which waited for: 2 -> 0; matrix products, arithmetic and copies ran while one was open for 0% -> 0% of each run, Pallas kernels for 0% -> 0%
where the time goes in v1:
time: 170 us; the launch traced here: 169 us
  Pallas kernels  157 us (92%)
  local copies, waits for them, and re-layouts  5.86 us (3%)
  other arithmetic  4.78 us (3%)
    pallas_call x1, Pallas kernels, products_of(): pl.pallas_call(kernel, out_shape=(jax.ShapeDtypeStruct((FEAT, 14 * LANE),...  157 us
    unnamed x12, local copies, waits for them, and re-layouts  5.34 us
    min x1, other arithmetic, body(): jnp.clip(new_moment / jnp.maximum(curvature_scale * new_curvature, ratio_...  4.78 us

profile of v1, /device:TPU:1, one launch (start us, length us, event | category | flops | bytes accessed | tf_op | source)
XLA Modules:
  0.0 169.3 jit_solution(14650078746341885792)
XLA Ops:
  0.6 0.0 copy-start
  0.6 1.2 copy-done
  1.8 0.0 copy-start.1
  1.8 1.2 copy-done.1
  3.0 0.0 copy-start.2
  3.0 1.2 copy-done.2
  4.2 0.0 copy-start.3
  4.2 0.9 copy-done.3
  5.1 0.0 copy-start.4
  5.1 0.9 copy-done.4
  6.0 0.0 copy-start.5
  6.0 157.3 %shard_map.94 = (bf16[256,1792]{1,0:T(8,128)(2,1)S(1)}, bf16[256,1792]{1,0:T(8,128)(2,1)S(1)}, f32[8,128]{1,0:T(8,128)S(1)}) custom-call(bf16[192,256]{1,0:T(8,128)(2,1)S(1)} %copy-done.4, bf16[48,1792]{1,0:T(8,128)(2,1)S(1)} %copy-done.3, bf16[256,1792]{1,0:T(8,128)(2,1)S(1)} %copy-done.1, bf16[256,1792]{1,0:T(8,128)(2,1)S(1)} %copy-done.2, ...), custom_call_target="tpu_custom_call" | custom-call | tf_op jit(solution)/shard_map/pallas_call | solution.py:396
  163.3 0.5 slice.3
  164.5 0.0 copy-done.5
  164.5 4.8 %divide_clamp_fusion = (f32[256,1792]{1,0:T(8,128)}, f32[256,1792]{1,0:T(8,128)}, f32[256,1792]{1,0:T(8,128)}) fusion(bf16[256,1792]{1,0:T(8,128)(2,1)S(1)} %get-tuple-element.8, bf16[256,1792]{1,0:T(8,128)(2,1)S(1)} %copy-done, f32[]{:T(128)} %bitcast.1, f32[256,1792]{1,0:T(8,128)S(1)} %copy-done.5, bf16[256,1792]{1,0:T(8,128)(2,1)S(1)} %get-tuple-element.7, ...), kind=kLoop, calls=%fused_computation.6 | loop fusion | flops 7798784 | bytes 11927560 | tf_op jit(solution)/shard_map/jit(clip)/min | solution.py:438
Async XLA Ops:
  0.6 1.2 copy-start
  1.8 1.2 copy-start.1
  3.0 1.2 copy-start.2
  4.2 0.9 copy-start.3
  5.1 0.9 copy-start.4
  6.0 158.5 %copy-start.5 = (f32[256,1792]{1,0:T(8,128)S(1)}, f32[256,1792]{1,0:T(8,128)}, u32[]{:S(2)}) copy-start(f32[256,1792]{1,0:T(8,128)} %param.13) | copy-start | bytes 5505028

commit v2 on v0

v2 whole, which is shorter than its diff:
```python
import functools

import jax
import jax.numpy as jnp
from jax import lax
from jax.experimental import pallas as pl
from jax.experimental.pallas import tpu as pltpu
from jax.sharding import PartitionSpec as P

D = 8192
FF = 14336

moment_decay = 0.9
curvature_decay = 0.99
curvature_scale = 2.0
ratio_floor = 0.05
mean_eps = 1e-06

NX, NY, NZ = 4, 4, 8
ROWS = 192
HALF = 96
FEAT = 256
DEPTH = NY * FEAT
LANE = 128
PAIR = 2 * LANE
TILES = 4

BF = jnp.bfloat16
F32 = jnp.float32


def first_part(gate_pre, up_value, upstream):
    sigmoid_val = jax.nn.sigmoid(gate_pre)
    first_deriv = sigmoid_val * (1.0 + gate_pre * (1.0 - sigmoid_val))
    return (upstream.astype(F32) * up_value * first_deriv).astype(BF)


def second_part(gate_pre, up_value, tangent, upstream):
    sigmoid_val = jax.nn.sigmoid(gate_pre)
    second_deriv = sigmoid_val * (1.0 - sigmoid_val) * (2.0 + gate_pre * (1.0 - 2.0 * sigmoid_val))
    return (upstream.astype(F32) * up_value * second_deriv * tangent).astype(BF)


def code4(val):
    return ((val * jnp.abs(val)) * (val * val)).astype(BF)


def decode4(coded):
    val = coded.astype(F32)
    root = lax.rsqrt(jnp.maximum(jnp.abs(val), 1e-36))
    return val * root * root * lax.rsqrt(root)


def code2(val):
    return (val * jnp.abs(val)).astype(BF)


def decode2(coded):
    val = coded.astype(F32)
    return val * lax.rsqrt(jnp.maximum(jnp.abs(val), 1e-36))


STEPS = (
    "U00", "V1", "U10", "U01", "U11", "V2", "U20", "U02", "V3", "U30", "U12", "U21", "U31", "U03", "U13",
    "V4", "V5", "T10", "U22", "U32", "T00", "T11", "U04", "U14", "G00", "T01", "U23", "U33", "T12", "G01",
    "T02", "U24", "U34", "G10", "T13", "G02", "T03", "G11", "T14", "H10", "G03", "T04", "G12", "G04", "H00",
    "P0", "H11", "G13", "H12", "G14", "H01", "P1", "S0", "H13", "H02", "H14", "P3", "H03", "S1", "H04",
    "P2", "S2", "S3",
)


def kernel(
    tok_in, hid_in, gate_in, up_in, probe_in,
    grad_out, curv_out, squares_out,
    tok, wsrc, wu, wt, hid, part_sum, totals, rs_out, rs_in, rows, outb, sq, sq_z, sq_y, sq_t,
    tok_l, ty_s, ty_r, tx_s, tx_r, tc_s, tc_r, src_l, wu_l, wu_s, wu_r, wt_l, wt_s, wt_r,
    hid_l, hid_s, hid_r, rs_s, rs_r, ag_s, ag_r, gr_l, gr_s, gr_r, sq_s, sq_r,
):
    tp, dp = lax.axis_index("tp"), lax.axis_index("dp")
    x, c = lax.div(tp, 2), lax.rem(tp, 2)
    z, y = lax.div(dp, NY), lax.rem(dp, NY)

    def mod(val, n):
        return lax.rem(val + n, n)

    def at_y(yy):
        return {"dp": z * NY + yy}

    def at_z(zz):
        return {"dp": zz * NY + y}

    def at_tp(tt):
        return {"tp": tt}

    def first_tile(yy):
        return lax.div(7 * yy + 1 - c, 2)

    def four(yy):
        return lax.rem(yy + c, 2) == 0

    four_here, three_here = four(y), lax.rem(y + c, 2) == 1

    def one(yy, t):
        return four(yy) if t == TILES - 1 else None

    def widths(yy, p):
        if p == 0:
            return ((None, PAIR),)
        return ((four(yy), PAIR), (lax.rem(yy + c, 2) == 1, LANE))

    def when(cond, fn):
        if cond is None:
            fn()
        else:
            pl.when(cond)(fn)

    def lanes(start, size):
        return pl.ds(pl.multiple_of(start, LANE), size)

    def tile_of(yy, t, size=LANE):
        return lanes((first_tile(yy) + t) * LANE, size)

    def feat(yy):
        return lanes(yy * FEAT, FEAT)

    def remote(src, dst, s_sem, r_sem, dev):
        return pltpu.make_async_remote_copy(
            src_ref=src, dst_ref=dst, send_sem=s_sem, recv_sem=r_sem,
            device_id=dev, device_id_type=pl.DeviceIdType.MESH,
        )

    def send(cond, *args):
        when(cond, remote(*args).start)

    def landed(dst, r_sem):
        remote(dst, dst, r_sem, r_sem, at_tp(tp)).wait_recv()

    def gone(src, s_sem):
        remote(src, src, s_sem, s_sem, at_tp(tp)).wait_send()

    tok_own = pltpu.make_async_copy(tok_in, tok.at[tp, :, feat(y)], tok_l)
    tok_own.start()
    weights = (gate_in, up_in, probe_in)
    staged = [pltpu.make_async_copy(weights[a], wsrc.at[a], src_l.at[a]) for a in range(3)]
    for copy in staged:
        copy.start()
    my_toks = pl.ds(pl.multiple_of(y * 48, 48), 48)

    def hid_own(p, size):
        return pltpu.make_async_copy(
            hid_in.at[:, tile_of(y, 2 * p, size)],
            hid.at[p, my_toks, pl.ds(0, size)],
            hid_l.at[p],
        )

    for p in range(2):
        for cond, size in widths(y, p):
            when(cond, hid_own(p, size).start)

    barrier = pltpu.get_barrier_semaphore()
    peers = [at_y(mod(y + r, NY)) for r in range(1, NY)]
    peers += [at_z(mod(z + r, NZ)) for r in range(1, NZ)]
    peers += [at_tp(mod(tp + r, 8)) for r in range(1, 8)]
    for dev in peers:
        pl.semaphore_signal(barrier, inc=1, device_id=dev, device_id_type=pl.DeviceIdType.MESH)
    pl.semaphore_wait(barrier, len(peers))

    x_next = (mod(tp + 2, 8), mod(tp - 2, 8))
    far = mod(tp + 4, 8)
    other = tp + 1 - 2 * c

    def x_send(blk, r, d, slot):
        ref = tok.at[blk, :, feat(mod(y - r, NY))]
        send(None, ref, ref, tx_s, tx_r.at[slot, r], at_tp(x_next[d]))

    def x_landed(blk, r, slot):
        landed(tok.at[blk, :, feat(mod(y - r, NY))], tx_r.at[slot, r])

    def core_send(blk):
        send(None, tok.at[blk], tok.at[blk], tc_s, tc_r.at[blk], at_tp(other))

    for r in range(1, NY):
        send(None, tok_in, tok.at[tp, :, feat(y)], ty_s, ty_r.at[r], at_y(mod(y + r, NY)))
    tok_own.wait()
    for d in range(2):
        x_send(tp, 0, d, d)
    for copy in staged:
        copy.wait()

    def wu_own(t):
        src, dst = wsrc.at[pl.ds(0, 2), :, tile_of(y, t)], wu.at[t, :, feat(y), :]
        return pltpu.make_async_copy(src, dst, wu_l.at[t])

    def wt_own(p, size):
        src, dst = wsrc.at[2, :, tile_of(y, 2 * p, size)], wt.at[p, feat(y), pl.ds(0, size)]
        return pltpu.make_async_copy(src, dst, wt_l.at[p])

    def send_weights(i):
        for r in (2, 1, 3):
            yy = mod(y + r, NY)
            if i < TILES:
                src, dst = wsrc.at[pl.ds(0, 2), :, tile_of(yy, i)], wu.at[i, :, feat(y), :]
                send(one(yy, i), src, dst, wu_s.at[i], wu_r.at[i, r], at_y(yy))
            else:
                p = i - TILES
                for cond, size in widths(yy, p):
                    src = wsrc.at[2, :, tile_of(yy, 2 * p, size)]
                    dst = wt.at[p, feat(y), pl.ds(0, size)]
                    send(cond, src, dst, wt_s.at[p], wt_r.at[p, r], at_y(yy))
        if i < TILES:
            when(one(y, i), wu_own(i).start)
        else:
            for cond, size in widths(y, i - TILES):
                when(cond, wt_own(i - TILES, size).start)

    def wait_weights(i):
        if i < TILES:

            def go():
                wu_own(i).wait()
                for r in range(1, NY):
                    landed(wu.at[i, :, feat(mod(y - r, NY)), :], wu_r.at[i, r])

            when(one(y, i), go)
            return
        p = i - TILES
        for cond, size in widths(y, p):

            def go():
                wt_own(p, size).wait()
                for r in range(1, NY):
                    landed(wt.at[p, feat(mod(y - r, NY)), pl.ds(0, size)], wt_r.at[p, r])

            when(cond, go)

    def send_hidden(p):
        for r in range(1, NY):
            yy = mod(y + r, NY)
            for cond, size in widths(yy, p):
                src = hid_in.at[:, tile_of(yy, 2 * p, size)]
                dst = hid.at[p, my_toks, pl.ds(0, size)]
                send(cond, src, dst, hid_s.at[p, r], hid_r.at[p, r], at_y(yy))

    def wait_hidden(p):
        for cond, size in widths(y, p):

            def go():
                hid_own(p, size).wait()
                for r in range(1, NY):
                    toks = pl.ds(pl.multiple_of(mod(y - r, NY) * 48, 48), 48)
                    landed(hid.at[p, toks, pl.ds(0, size)], hid_r.at[p, r])

            when(cond, go)

    for r in (1, 3, 2):
        landed(tok.at[tp, :, feat(mod(y - r, NY))], ty_r.at[r])
        for d in range(2):
            x_send(tp, r, d, d)
    send_weights(0)
    core_send(tp)
    for d, r in ((0, 0), (0, 1), (1, 3), (1, 2)):
        x_landed(x_next[1 - d], r, d)
        x_send(x_next[1 - d], r, d, 2)
    for d, rest in ((0, (3, 2)), (1, (0, 1))):
        for r in rest:
            x_landed(x_next[1 - d], r, d)
        core_send(x_next[1 - d])
    send_weights(1)

    def far_tokens():
        for r in (0, 1, 3, 2):
            x_landed(far, r, 2)
        core_send(far)

    far_first = lax.div(mod(z + 4, NZ), 2) == lax.div(far, 2)
    far_later = lax.div(mod(z + 4, NZ), 2) != lax.div(far, 2)

    def wait_block(blk):
        pl.when(lax.rem(blk, 2) != c)(lambda: landed(tok.at[blk], tc_r.at[blk]))

    z_next = (mod(z + 1, NZ), mod(z - 1, NZ))

    def unit_widths(u):
        if u >= TILES:
            return widths(y, u - TILES)
        return ((one(y, u), PAIR),)

    def hop(s):
        return pl.ds(0, 1) if s == 0 else pl.ds(2 * s - 1, 2)

    def dots(u, s):
        if s in (0, 4):
            blks = (mod(z + 4 - s, NZ),)
        else:
            blks = (mod(z + 4 - s, NZ), mod(z - 4 + s, NZ))
        for d, blk in enumerate(blks):
            if u == 0:
                wait_block(blk)
            for cond, size in unit_widths(u):

                def go():
                    if u < TILES:
                        wide = jnp.concatenate([wu[u, a] for a in range(2)], axis=1)
                    else:
                        wide = wt[u - TILES, :, pl.ds(0, size)]
                    val = jnp.dot(tok[blk], wide, preferred_element_type=F32)
                    part_sum[u, d, :, :, pl.ds(0, size)] = val.reshape(2, HALF, size)

                when(cond, go)

    def rs_step(u, s):
        if s == 0:
            dots(u, 0)
        for d in range(2):
            for cond, size in unit_widths(u):
                cols = pl.ds(0, size)

                def go():
                    if s == 0:
                        rs_out[u, d, 0, :, cols] = code4(part_sum[u, 0, d, :, cols])
                        return
                    if s == 1:
                        got, at = rs_in.at[u, d, pl.ds(0, 1), :, cols], pl.ds(d, 1)
                    else:
                        got, at = rs_in.at[u, d, hop(s - 1), :, cols], pl.ds(0, 2)
                    landed(got, rs_r.at[u, d, s - 1])
                    part_sum[u, d, at, :, cols] = part_sum[u, d, at, :, cols] + decode4(got[...])
                    rs_out[u, d, hop(s), :, cols] = code4(part_sum[u, d, :, :, cols])

                when(cond, go)
                src, dst = rs_out.at[u, d, hop(s), :, cols], rs_in.at[u, d, hop(s), :, cols]
                send(cond, src, dst, rs_s.at[u], rs_r.at[u, d, s], at_z(z_next[d]))
        if u == 0 and s == 0:
            pl.when(far_later)(far_tokens)
        dots(u, s + 1)

    def rs_total(u, size):
        cols = pl.ds(0, size)
        val = part_sum[u, 0, :, :, cols]
        for d in range(2):
            got = rs_in.at[u, d, hop(3), :, cols]
            landed(got, rs_r.at[u, d, 3])
            val = val + decode4(got[...])
        return val.reshape(ROWS, size)

    def tile_cols(t):
        return pl.ds((t % 2) * LANE, LANE)

    def last_gate_up(t):
        if t % 2 == 0:
            wait_hidden(t // 2)

        def go():
            val = rs_total(t, PAIR)
            totals[t] = val
            rows[t // 2, z, :, tile_cols(t)] = first_part(
                val[:, :LANE], val[:, LANE:], hid[t // 2, :, tile_cols(t)]
            )

        when(one(y, t), go)

    def last_tangent(p):
        for cond, size in widths(y, p):

            def go():
                val = rs_total(TILES + p, size)
                for i in range(size // LANE):
                    gate_up, cols = totals[2 * p + i], tile_cols(i)
                    rows[2 + p, z, :, cols] = second_part(
                        gate_up[:, :LANE], gate_up[:, LANE:],
                        val[:, i * LANE : (i + 1) * LANE], hid[p, :, cols],
                    )

            when(cond, go)

    def ag_part(s, d):
        return pl.ds(0, ROWS) if s < 3 else pl.ds(d * HALF, HALF)

    def ag_step(u, s):
        for d in range(2):
            back = s if d == 0 else -s
            blk = mod(z - back, NZ)
            for cond, size in widths(y, u % 2):
                cols = pl.ds(0, size)
                if s > 0:
                    got = rows.at[u, blk, ag_part(s - 1, d), cols]
                    when(cond, lambda: landed(got, ag_r.at[u, d, s - 1]))
                if s < 4:
                    ref = rows.at[u, blk, ag_part(s, d), cols]
                    send(cond, ref, ref, ag_s.at[u], ag_r.at[u, d, s], at_z(z_next[d]))

    outs = (grad_out, curv_out)
    sq[...] = jnp.zeros_like(sq)

    def products(u):
        a, p = u // 2, u % 2
        for i, j in enumerate((2, 1, 3, 0)):
            yy = mod(y + j, NY)
            for cond, size in widths(y, p):
                cols = pl.ds(0, size)

                def go():
                    val = lax.dot_general(
                        tok[:, :, feat(yy)].reshape(NZ * ROWS, FEAT),
                        rows[u, :, :, cols].reshape(NZ * ROWS, size),
                        (((0,), (0,)), ((), ())), preferred_element_type=F32,
                    )
                    if a == 0:
                        squared = jnp.sum((val * val).reshape(FEAT // 8, 8, size), axis=0)
                        for k in range(size // LANE):
                            sq[...] += squared[:, k * LANE : (k + 1) * LANE]
                        outb[u, i, :, cols] = val.astype(BF)
                    else:
                        outb[u, i, :, cols] = code2(val)

                when(cond, go)
                src, dst = outb.at[u, i, :, cols], outs[a].at[:, tile_of(y, 2 * p, size)]
                if j:
                    send(cond, src, dst, gr_s.at[u], gr_r.at[u, j], at_y(yy))
                else:
                    when(cond, pltpu.make_async_copy(src, dst, gr_l.at[u]).start)

    stages = ((sq_z, NZ, z, at_z, 0), (sq_y, NY, y, at_y, 8), (sq_t, 8, tp, at_tp, 12))

    def sum_stage(i):
        if i > 0:
            buf, n, me, _, base = stages[i - 1]
            for r in range(1, n):
                landed(buf.at[mod(me - r, n)], sq_r.at[base + r])
            sq[...] = jnp.sum(buf[...], axis=0)
        if i < len(stages):
            buf, n, me, dev_at, base = stages[i]
            buf[me] = sq[...]
            for r in range(1, n):
                dst = buf.at[me]
                send(None, dst, dst, sq_s.at[i], sq_r.at[base + r], dev_at(mod(me + r, n)))

    pl.when(far_first)(far_tokens)
    wait_weights(0)
    send_hidden(0)
    send_weights(2)
    for step in STEPS:
        kind, i = step[0], int(step[1])
        s = int(step[2:] or 0)
        if kind == "V":
            wait_weights(i)
            if i + 2 < TILES + 2:
                send_weights(i + 2)
            if i == 1:
                send_hidden(1)
        elif kind == "U":
            last_gate_up(i) if s == 4 else rs_step(i, s)
        elif kind == "T":
            last_tangent(i) if s == 4 else rs_step(TILES + i, s)
        elif kind == "G":
            ag_step(i, s)
        elif kind == "H":
            ag_step(2 + i, s)
        elif kind == "P":
            products(i)
        else:
            sum_stage(i)
    squares_out[...] = jnp.broadcast_to(jnp.sum(sq[...]), (8, LANE))

    for u in range(4):
        a, p = u // 2, u % 2
        for j in range(1, NY):
            yy = mod(y - j, NY)
            for cond, size in widths(yy, p):
                got = outs[a].at[:, tile_of(yy, 2 * p, size)]
                when(cond, lambda: landed(got, gr_r.at[u, j]))
        for cond, size in widths(y, p):
            cols = pl.ds(0, size)

            def go():
                src, dst = outb.at[u, 3, :, cols], outs[a].at[:, tile_of(y, 2 * p, size)]
                pltpu.make_async_copy(src, dst, gr_l.at[u]).wait()
                gone(outb.at[u, pl.ds(0, 3), :, cols], gr_s.at[u])
                gone(rows.at[u, pl.ds(0, 7), :, cols], ag_s.at[u])

            when(cond, go)
    for u in range(6):
        for cond, size in unit_widths(u):
            when(cond, lambda: gone(rs_out.at[u, :, :, :, pl.ds(0, size)], rs_s.at[u]))
    gone(tok.at[0, :, pl.ds(0, 3 * FEAT)], ty_s)
    gone(tok.at[pl.ds(0, 3)], tx_s)
    gone(tok.at[pl.ds(0, 4)], tc_s)
    for t in range(TILES - 1):
        gone(wu.at[t, :, pl.ds(0, 3 * FEAT), :], wu_s.at[t])
    gone(wt.at[0, pl.ds(0, 3 * FEAT), :], wt_s.at[0])
    for cond, n in ((four_here, 2), (three_here, 4)):
        when(cond, lambda: gone(wu.at[TILES - 1, :, pl.ds(0, n * FEAT // 2), :], wu_s.at[TILES - 1]))
        when(cond, lambda: gone(wt.at[1, pl.ds(0, FEAT * (n + 6) // 4), :], wt_s.at[1]))
    for r in range(1, NY):
        yy = mod(y + r, NY)
        for p in range(2):
            for cond, size in widths(yy, p):
                when(cond, lambda: gone(hid.at[p, my_toks, pl.ds(0, size)], hid_s.at[p, r]))
    for i, (buf, n, _, _, _) in enumerate(stages):
        gone(buf.at[pl.ds(0, n - 1)], sq_s.at[i])


def products_of(tokens, hidden_grad, gate_weight, up_weight, probe):
    dma = pltpu.SemaphoreType.DMA
    hbm = pl.BlockSpec(memory_space=pl.ANY)
    far = pl.BlockSpec(memory_space=pltpu.HBM)
    return pl.pallas_call(
        kernel,
        out_shape=(
            jax.ShapeDtypeStruct((FEAT, 14 * LANE), BF),
            jax.ShapeDtypeStruct((FEAT, 14 * LANE), BF),
            jax.ShapeDtypeStruct((8, LANE), F32),
        ),
        in_specs=[far] * 5,
        out_specs=(hbm, hbm, pl.BlockSpec(memory_space=pltpu.VMEM)),
        scratch_shapes=[
            pltpu.VMEM((8, ROWS, DEPTH), BF),
            pltpu.VMEM((3, FEAT, 14 * LANE), BF),
            pltpu.VMEM((TILES, 2, DEPTH, LANE), BF),
            pltpu.VMEM((2, DEPTH, PAIR), BF),
            pltpu.VMEM((2, ROWS, PAIR), BF),
            pltpu.VMEM((6, 2, 2, HALF, PAIR), F32),
            pltpu.VMEM((TILES, ROWS, PAIR), F32),
            pltpu.VMEM((6, 2, 7, HALF, PAIR), BF),
            pltpu.VMEM((6, 2, 7, HALF, PAIR), BF),
            pltpu.VMEM((4, NZ, ROWS, PAIR), BF),
            pltpu.VMEM((4, NY, FEAT, PAIR), BF),
            pltpu.VMEM((8, LANE), F32),
            pltpu.VMEM((NZ, 8, LANE), F32),
            pltpu.VMEM((NY, 8, LANE), F32),
            pltpu.VMEM((8, 8, LANE), F32),
            dma, dma, dma((NY,)), dma, dma((3, NY)), dma, dma((8,)), dma((3,)),
            dma((TILES,)), dma((TILES,)), dma((TILES, NY)), dma((2,)), dma((2,)), dma((2, NY)),
            dma((2,)), dma((2, NY)), dma((2, NY)),
            dma((6,)), dma((6, 2, 4)), dma((4,)), dma((4, 2, 4)),
            dma((4,)), dma((4,)), dma((4, NY)), dma((3,)), dma((20,)),
        ],
        compiler_params=pltpu.CompilerParams(
            collective_id=0, has_side_effects=True, vmem_limit_bytes=62 * 1024 * 1024
        ),
    )(tokens, hidden_grad, gate_weight, up_weight, probe)


def finish(squares, grad, curv, probe, moment, curvature, moment_out, curvature_out, update_out):
    factor = jnp.minimum(1.0, lax.rsqrt(squares[0:1, 0:1] / (D * FF) + mean_eps))
    new_moment = moment_decay * moment[...] + (1.0 - moment_decay) * factor * grad[...].astype(F32)
    new_curvature = curvature_decay * curvature[...] + (
        1.0 - curvature_decay
    ) * factor * probe[...].astype(F32) * decode2(curv[...])
    moment_out[...] = new_moment
    curvature_out[...] = new_curvature
    update_out[...] = jnp.clip(
        new_moment / jnp.maximum(curvature_scale * new_curvature, ratio_floor), -1.0, 1.0
    )


def body(tokens, hidden_grad, gate_weight, up_weight, probe, moment, curvature):
    gradient, curv_coded, squares = products_of(tokens, hidden_grad, gate_weight, up_weight, probe)
    part = pl.BlockSpec((64, 14 * LANE), lambda i: (i, 0))
    return pl.pallas_call(
        finish,
        grid=(FEAT // 64,),
        out_shape=[jax.ShapeDtypeStruct((FEAT, 14 * LANE), F32)] * 3,
        in_specs=[pl.BlockSpec((8, LANE), lambda i: (0, 0))] + [part] * 5,
        out_specs=[part] * 3,
        compiler_params=pltpu.CompilerParams(vmem_limit_bytes=62 * 1024 * 1024),
    )(squares, gradient, curv_coded, probe, moment, curvature)


def solution(mesh):
    placed = (
        P("tp", "dp"),
        P("dp", "tp"),
        P("dp", "tp"),
        P("dp", "tp"),
        P("dp", "tp"),
        P("dp", "tp"),
        P("dp", "tp"),
    )
    return jax.shard_map(
        body,
        mesh=mesh,
        in_specs=placed,
        out_specs=(P("dp", "tp"), P("dp", "tp"), P("dp", "tp")),
        check_vma=False,
    )
```

time: 604 us -> 125 us (0.21)
  waiting for transfers between devices: 420 us -> 0 us
  Pallas kernels: 0 us -> 124 us
  blocking collectives: 91.7 us -> 0 us
  local copies, waits for them, and re-layouts: 47.4 us -> 0 us
  matrix products: 20.7 us -> 0 us
  between operations: 14.8 us -> 0.64 us
  other arithmetic: 8.61 us -> 0 us
    reduce_scatter x1 -> x0, waiting for transfers between devices: 311 us -> none  [body(): lax.psum_scatter(row_products(features, weights), 'dp', scatter_dimension...]
    pallas_call x0 -> x2, Pallas kernels: none -> 124 us  [the longest x1 118 us: products_of(): pl.pallas_call(kernel, out_shape=(jax.ShapeDtypeStruct((FEAT, 14 * LANE),...]
    all_gather x1 -> x0, waiting for transfers between devices: 109 us -> none  [body(): lax.all_gather(jnp.concatenate([grad_rows, hess_rows], axis=1), 'dp', axi...]
    psum x1 -> x0, blocking collectives: 74.9 us -> none  [body(): squares = lax.psum(jnp.sum(gradient * gradient), ('tp', 'dp'))]
    unnamed x15 -> x0, local copies, waits for them, and re-layouts: 47.4 us -> none
    dot_general x2 -> x0, matrix products: 20.7 us -> none  [the longest x1 14.9 us: row_products(): return jnp.dot(features, weights, preferred_element_type=jnp.float32)]
    all_gather x1 -> x0, blocking collectives: 16.8 us -> none  [body(): features = lax.all_gather(tokens, 'tp', axis=0, tiled=True)]
  transfers between devices with their start and end apart: 2 -> 0, of which waited for: 2 -> 0; matrix products, arithmetic and copies ran while one was open for 0% -> 0% of each run, Pallas kernels for 0% -> 0%
where the time goes in v2:
time: 125 us; the launch traced here: 124 us
  Pallas kernels  124 us (99%)
    pallas_call x1, Pallas kernels, products_of(): pl.pallas_call(kernel, out_shape=(jax.ShapeDtypeStruct((FEAT, 14 * LANE),...  118 us
    pallas_call x1, Pallas kernels, body(): pl.pallas_call(finish, grid=(FEAT // 64,), out_shape=[jax.ShapeDtypeStruc...  6.03 us

profile of v2, /device:TPU:1, one launch (start us, length us, event | category | flops | bytes accessed | tf_op | source)
XLA Modules:
  0.0 124.4 jit_solution(8187913122062642252)
XLA Ops:
  0.6 117.7 %shard_map.94 = (bf16[256,1792]{1,0:T(8,128)(2,1)}, bf16[256,1792]{1,0:T(8,128)(2,1)}, f32[8,128]{1,0:T(8,128)}) custom-call(bf16[192,256]{1,0:T(8,128)(2,1)} %tok_in.1, bf16[48,1792]{1,0:T(8,128)(2,1)} %hid_in.1, bf16[256,1792]{1,0:T(8,128)(2,1)} %gate_in.1, bf16[256,1792]{1,0:T(8,128)(2,1)} %up_in.1, bf16[256,1792]{1,0:T(8,128)(2,1)} %probe.1), custom_call_target="tpu_custom_call" | custom-call | tf_op jit(solution)/shard_map/pallas_call | solution.py:507
  118.4 6.0 %shard_map.95 = (f32[256,1792]{1,0:T(8,128)}, f32[256,1792]{1,0:T(8,128)}, f32[256,1792]{1,0:T(8,128)}) custom-call(f32[8,128]{1,0:T(8,128)} %get-tuple-element.6.squares, bf16[256,1792]{1,0:T(8,128)(2,1)} %get-tuple-element.7.grad, bf16[256,1792]{1,0:T(8,128)(2,1)} %get-tuple-element.8.curv, bf16[256,1792]{1,0:T(8,128)(2,1)} %probe.1, f32[256,1792]{1,0:T(8,128)} %moment.1, ...), custom_call_target="tpu_custom_call" | custom-call | tf_op jit(solution)/shard_map/pallas_call | solution.py:560

commit v3 on v2

--- a/solution.py
+++ b/solution.py
@@ -62,11 +62,12 @@
 
 STEPS = (
     "U00", "V1", "U10", "U01", "U11", "V2", "U20", "U02", "V3", "U30", "U12", "U21", "U31", "U03", "U13",
-    "V4", "V5", "T10", "U22", "U32", "T00", "T11", "U04", "U14", "G00", "T01", "U23", "U33", "T12", "G01",
-    "T02", "U24", "U34", "G10", "T13", "G02", "T03", "G11", "T14", "H10", "G03", "T04", "G12", "G04", "H00",
-    "P0", "H11", "G13", "H12", "G14", "H01", "P1", "S0", "H13", "H02", "H14", "P3", "H03", "S1", "H04",
+    "V4", "V5", "T10", "U22", "T00", "U32", "T11", "U04", "U14", "G00", "T01", "U23", "U33", "T12", "G01",
+    "T02", "U24", "U34", "G10", "T13", "G02", "T03", "G11", "T14", "H10", "G03", "T04", "G12", "H11", "G04",
+    "H00", "P0", "G13", "H12", "G14", "H01", "P1", "S0", "H13", "H02", "H14", "P3", "H03", "S1", "H04",
     "P2", "S2", "S3",
 )
+ENDS = tuple(int(step[1]) for step in STEPS if step[0] == "P")
 
 
 def kernel(
@@ -179,7 +180,7 @@
     def core_send(blk):
         send(None, tok.at[blk], tok.at[blk], tc_s, tc_r.at[blk], at_tp(other))
 
-    for r in range(1, NY):
+    for r in (1, 3, 2):
         send(None, tok_in, tok.at[tp, :, feat(y)], ty_s, ty_r.at[r], at_y(mod(y + r, NY)))
     tok_own.wait()
     for d in range(2):
@@ -324,8 +325,11 @@
                     else:
                         got, at = rs_in.at[u, d, hop(s - 1), :, cols], pl.ds(0, 2)
                     landed(got, rs_r.at[u, d, s - 1])
-                    part_sum[u, d, at, :, cols] = part_sum[u, d, at, :, cols] + decode4(got[...])
-                    rs_out[u, d, hop(s), :, cols] = code4(part_sum[u, d, :, :, cols])
+                    val = part_sum[u, d, at, :, cols] + decode4(got[...])
+                    if s == 1:
+                        part_sum[u, d, at, :, cols] = val
+                        val = part_sum[u, d, :, :, cols]
+                    rs_out[u, d, hop(s), :, cols] = code4(val)
 
                 when(cond, go)
                 src, dst = rs_out.at[u, d, hop(s), :, cols], rs_in.at[u, d, hop(s), :, cols]
@@ -462,26 +466,6 @@
             sum_stage(i)
     squares_out[...] = jnp.broadcast_to(jnp.sum(sq[...]), (8, LANE))
 
-    for u in range(4):
-        a, p = u // 2, u % 2
-        for j in range(1, NY):
-            yy = mod(y - j, NY)
-            for cond, size in widths(yy, p):
-                got = outs[a].at[:, tile_of(yy, 2 * p, size)]
-                when(cond, lambda: landed(got, gr_r.at[u, j]))
-        for cond, size in widths(y, p):
-            cols = pl.ds(0, size)
-
-            def go():
-                src, dst = outb.at[u, 3, :, cols], outs[a].at[:, tile_of(y, 2 * p, size)]
-                pltpu.make_async_copy(src, dst, gr_l.at[u]).wait()
-                gone(outb.at[u, pl.ds(0, 3), :, cols], gr_s.at[u])
-                gone(rows.at[u, pl.ds(0, 7), :, cols], ag_s.at[u])
-
-            when(cond, go)
-    for u in range(6):
-        for cond, size in unit_widths(u):
-            when(cond, lambda: gone(rs_out.at[u, :, :, :, pl.ds(0, size)], rs_s.at[u]))
     gone(tok.at[0, :, pl.ds(0, 3 * FEAT)], ty_s)
     gone(tok.at[pl.ds(0, 3)], tx_s)
     gone(tok.at[pl.ds(0, 4)], tc_s)
@@ -498,6 +482,28 @@
                 when(cond, lambda: gone(hid.at[p, my_toks, pl.ds(0, size)], hid_s.at[p, r]))
     for i, (buf, n, _, _, _) in enumerate(stages):
         gone(buf.at[pl.ds(0, n - 1)], sq_s.at[i])
+    for u in range(6):
+        for cond, size in unit_widths(u):
+            when(cond, lambda: gone(rs_out.at[u, :, :, :, pl.ds(0, size)], rs_s.at[u]))
+    for u in range(4):
+        for cond, size in widths(y, u % 2):
+            when(cond, lambda: gone(rows.at[u, pl.ds(0, 7), :, pl.ds(0, size)], ag_s.at[u]))
+    for u in ENDS:
+        a, p = u // 2, u % 2
+        for cond, size in widths(y, p):
+            cols = pl.ds(0, size)
+
+            def go():
+                src, dst = outb.at[u, 3, :, cols], outs[a].at[:, tile_of(y, 2 * p, size)]
+                pltpu.make_async_copy(src, dst, gr_l.at[u]).wait()
+                gone(outb.at[u, pl.ds(0, 3), :, cols], gr_s.at[u])
+
+            when(cond, go)
+        for j in range(1, NY):
+            yy = mod(y - j, NY)
+            for cond, size in widths(yy, p):
+                got = outs[a].at[:, tile_of(yy, 2 * p, size)]
+                when(cond, lambda: landed(got, gr_r.at[u, j]))
 
 
 def products_of(tokens, hidden_grad, gate_weight, up_weight, probe):
@@ -556,10 +562,10 @@
 
 def body(tokens, hidden_grad, gate_weight, up_weight, probe, moment, curvature):
     gradient, curv_coded, squares = products_of(tokens, hidden_grad, gate_weight, up_weight, probe)
-    part = pl.BlockSpec((64, 14 * LANE), lambda i: (i, 0))
+    part = pl.BlockSpec((128, 14 * LANE), lambda i: (i, 0))
     return pl.pallas_call(
         finish,
-        grid=(FEAT // 64,),
+        grid=(FEAT // 128,),
         out_shape=[jax.ShapeDtypeStruct((FEAT, 14 * LANE), F32)] * 3,
         in_specs=[pl.BlockSpec((8, LANE), lambda i: (0, 0))] + [part] * 5,
         out_specs=[part] * 3,

time: 125 us -> 122 us (0.976)
  Pallas kernels: 124 us -> 122 us
    pallas_call x1, Pallas kernels: 118 us -> 116 us  [products_of(): pl.pallas_call(kernel, out_shape=(jax.ShapeDtypeStruct((FEAT, 14 * LANE),...]
where the time goes in v3:
time: 122 us
  Pallas kernels  122 us (100%)
    pallas_call x1, Pallas kernels, products_of(): pl.pallas_call(kernel, out_shape=(jax.ShapeDtypeStruct((FEAT, 14 * LANE),...  116 us
    pallas_call x1, Pallas kernels, body(): pl.pallas_call(finish, grid=(FEAT // 128,), out_shape=[jax.ShapeDtypeStru...  5.43 us

profile of v3, /device:TPU:1, one launch (start us, length us, event | category | flops | bytes accessed | tf_op | source)
XLA Modules:
  0.0 122.3 jit_solution(10124115718724540313)
XLA Ops:
  0.6 116.3 %shard_map.94 = (bf16[256,1792]{1,0:T(8,128)(2,1)}, bf16[256,1792]{1,0:T(8,128)(2,1)}, f32[8,128]{1,0:T(8,128)}) custom-call(bf16[192,256]{1,0:T(8,128)(2,1)} %tok_in.1, bf16[48,1792]{1,0:T(8,128)(2,1)} %hid_in.1, bf16[256,1792]{1,0:T(8,128)(2,1)} %gate_in.1, bf16[256,1792]{1,0:T(8,128)(2,1)} %up_in.1, bf16[256,1792]{1,0:T(8,128)(2,1)} %probe.1), custom_call_target="tpu_custom_call" | custom-call | tf_op jit(solution)/shard_map/pallas_call | solution.py:513
  116.9 5.4 %shard_map.95 = (f32[256,1792]{1,0:T(8,128)}, f32[256,1792]{1,0:T(8,128)}, f32[256,1792]{1,0:T(8,128)}) custom-call(f32[8,128]{1,0:T(8,128)} %get-tuple-element.6.squares, bf16[256,1792]{1,0:T(8,128)(2,1)} %get-tuple-element.7.grad, bf16[256,1792]{1,0:T(8,128)(2,1)} %get-tuple-element.8.curv, bf16[256,1792]{1,0:T(8,128)(2,1)} %probe.1, f32[256,1792]{1,0:T(8,128)} %moment.1, ...), custom_call_target="tpu_custom_call" | custom-call | tf_op jit(solution)/shard_map/pallas_call | solution.py:566

commit v4 on v3

--- a/solution.py
+++ b/solution.py
@@ -257,7 +257,8 @@
         landed(tok.at[tp, :, feat(mod(y - r, NY))], ty_r.at[r])
         for d in range(2):
             x_send(tp, r, d, d)
-    send_weights(0)
+        if r == 3:
+            send_weights(0)
     core_send(tp)
     for d, r in ((0, 0), (0, 1), (1, 3), (1, 2)):
         x_landed(x_next[1 - d], r, d)
@@ -309,10 +310,17 @@
 
                 when(cond, go)
 
+    def rs_send(u, d, at, sem):
+        for cond, size in unit_widths(u):
+            cols = pl.ds(0, size)
+            src, dst = rs_out.at[u, d, at, :, cols], rs_in.at[u, d, at, :, cols]
+            send(cond, src, dst, rs_s.at[u], rs_r.at[u, d, sem], at_z(z_next[d]))
+
     def rs_step(u, s):
         if s == 0:
             dots(u, 0)
         for d in range(2):
+            at = pl.ds(1 + d, 1) if s == 1 else hop(s)
             for cond, size in unit_widths(u):
                 cols = pl.ds(0, size)
 
@@ -320,23 +328,31 @@
                     if s == 0:
                         rs_out[u, d, 0, :, cols] = code4(part_sum[u, 0, d, :, cols])
                         return
-                    if s == 1:
-                        got, at = rs_in.at[u, d, pl.ds(0, 1), :, cols], pl.ds(d, 1)
+                    part = pl.ds(d, 1) if s == 1 else pl.ds(0, 2)
+                    if s == 2:
+                        landed(rs_in.at[u, d, pl.ds(1 + d, 1), :, cols], rs_r.at[u, d, 1])
+                        landed(rs_in.at[u, d, pl.ds(2 - d, 1), :, cols], rs_r.at[u, d, 4])
                     else:
-                        got, at = rs_in.at[u, d, hop(s - 1), :, cols], pl.ds(0, 2)
-                    landed(got, rs_r.at[u, d, s - 1])
-                    val = part_sum[u, d, at, :, cols] + decode4(got[...])
-                    if s == 1:
-                        part_sum[u, d, at, :, cols] = val
-                        val = part_sum[u, d, :, :, cols]
-                    rs_out[u, d, hop(s), :, cols] = code4(val)
+                        landed(rs_in.at[u, d, hop(s - 1), :, cols], rs_r.at[u, d, s - 1])
+                    val = part_sum[u, d, part, :, cols] + decode4(rs_in[u, d, hop(s - 1), :, cols])
+                    rs_out[u, d, at, :, cols] = code4(val)
 
                 when(cond, go)
-                src, dst = rs_out.at[u, d, hop(s), :, cols], rs_in.at[u, d, hop(s), :, cols]
-                send(cond, src, dst, rs_s.at[u], rs_r.at[u, d, s], at_z(z_next[d]))
+            rs_send(u, d, at, s)
         if u == 0 and s == 0:
             pl.when(far_later)(far_tokens)
         dots(u, s + 1)
+        if s > 0:
+            return
+        for d in range(2):
+            for cond, size in unit_widths(u):
+                cols = pl.ds(0, size)
+
+                def early():
+                    rs_out[u, d, 2 - d, :, cols] = code4(part_sum[u, d, 1 - d, :, cols])
+
+                when(cond, early)
+            rs_send(u, d, pl.ds(2 - d, 1), 4)
 
     def rs_total(u, size):
         cols = pl.ds(0, size)
@@ -538,7 +554,7 @@
             dma, dma, dma((NY,)), dma, dma((3, NY)), dma, dma((8,)), dma((3,)),
             dma((TILES,)), dma((TILES,)), dma((TILES, NY)), dma((2,)), dma((2,)), dma((2, NY)),
             dma((2,)), dma((2, NY)), dma((2, NY)),
-            dma((6,)), dma((6, 2, 4)), dma((4,)), dma((4, 2, 4)),
+            dma((6,)), dma((6, 2, 5)), dma((4,)), dma((4, 2, 4)),
             dma((4,)), dma((4,)), dma((4, NY)), dma((3,)), dma((20,)),
         ],
         compiler_params=pltpu.CompilerParams(

time: 122 us -> 121 us (level)
  Pallas kernels: 122 us -> 120 us
    pallas_call x1, Pallas kernels: 116 us -> 115 us  [products_of(): pl.pallas_call(kernel, out_shape=(jax.ShapeDtypeStruct((FEAT, 14 * LANE),...]
where the time goes in v4:
time: 121 us
  Pallas kernels  120 us (99%)
    pallas_call x1, Pallas kernels, products_of(): pl.pallas_call(kernel, out_shape=(jax.ShapeDtypeStruct((FEAT, 14 * LANE),...  115 us
    pallas_call x1, Pallas kernels, body(): pl.pallas_call(finish, grid=(FEAT // 128,), out_shape=[jax.ShapeDtypeStru...  5.43 us

profile of v4, /device:TPU:1, one launch (start us, length us, event | category | flops | bytes accessed | tf_op | source)
XLA Modules:
  0.0 120.8 jit_solution(16866978932132562975)
XLA Ops:
  0.6 114.7 %shard_map.94 = (bf16[256,1792]{1,0:T(8,128)(2,1)}, bf16[256,1792]{1,0:T(8,128)(2,1)}, f32[8,128]{1,0:T(8,128)}) custom-call(bf16[192,256]{1,0:T(8,128)(2,1)} %tok_in.1, bf16[48,1792]{1,0:T(8,128)(2,1)} %hid_in.1, bf16[256,1792]{1,0:T(8,128)(2,1)} %gate_in.1, bf16[256,1792]{1,0:T(8,128)(2,1)} %up_in.1, bf16[256,1792]{1,0:T(8,128)(2,1)} %probe.1), custom_call_target="tpu_custom_call" | custom-call | tf_op jit(solution)/shard_map/pallas_call | solution.py:529
  115.3 5.4 %shard_map.95 = (f32[256,1792]{1,0:T(8,128)}, f32[256,1792]{1,0:T(8,128)}, f32[256,1792]{1,0:T(8,128)}) custom-call(f32[8,128]{1,0:T(8,128)} %get-tuple-element.6.squares, bf16[256,1792]{1,0:T(8,128)(2,1)} %get-tuple-element.7.grad, bf16[256,1792]{1,0:T(8,128)(2,1)} %get-tuple-element.8.curv, bf16[256,1792]{1,0:T(8,128)(2,1)} %probe.1, f32[256,1792]{1,0:T(8,128)} %moment.1, ...), custom_call_target="tpu_custom_call" | custom-call | tf_op jit(solution)/shard_map/pallas_call | solution.py:582

commit v5 on v4

--- a/solution.py
+++ b/solution.py
@@ -263,11 +263,11 @@
     for d, r in ((0, 0), (0, 1), (1, 3), (1, 2)):
         x_landed(x_next[1 - d], r, d)
         x_send(x_next[1 - d], r, d, 2)
+    send_weights(1)
     for d, rest in ((0, (3, 2)), (1, (0, 1))):
         for r in rest:
             x_landed(x_next[1 - d], r, d)
         core_send(x_next[1 - d])
-    send_weights(1)
 
     def far_tokens():
         for r in (0, 1, 3, 2):

time: 121 us -> 121 us (level)
  no operation moved by 1% of the time
where the time goes in v5:
time: 121 us
  Pallas kernels  120 us (99%)
    pallas_call x1, Pallas kernels, products_of(): pl.pallas_call(kernel, out_shape=(jax.ShapeDtypeStruct((FEAT, 14 * LANE),...  115 us
    pallas_call x1, Pallas kernels, body(): pl.pallas_call(finish, grid=(FEAT // 128,), out_shape=[jax.ShapeDtypeStru...  5.43 us

profile of v5, /device:TPU:1, one launch (start us, length us, event | category | flops | bytes accessed | tf_op | source)
XLA Modules:
  0.0 120.9 jit_solution(3247208407021895200)
XLA Ops:
  0.6 114.8 %shard_map.94 = (bf16[256,1792]{1,0:T(8,128)(2,1)}, bf16[256,1792]{1,0:T(8,128)(2,1)}, f32[8,128]{1,0:T(8,128)}) custom-call(bf16[192,256]{1,0:T(8,128)(2,1)} %tok_in.1, bf16[48,1792]{1,0:T(8,128)(2,1)} %hid_in.1, bf16[256,1792]{1,0:T(8,128)(2,1)} %gate_in.1, bf16[256,1792]{1,0:T(8,128)(2,1)} %up_in.1, bf16[256,1792]{1,0:T(8,128)(2,1)} %probe.1), custom_call_target="tpu_custom_call" | custom-call | tf_op jit(solution)/shard_map/pallas_call | solution.py:529
  115.4 5.4 %shard_map.95 = (f32[256,1792]{1,0:T(8,128)}, f32[256,1792]{1,0:T(8,128)}, f32[256,1792]{1,0:T(8,128)}) custom-call(f32[8,128]{1,0:T(8,128)} %get-tuple-element.6.squares, bf16[256,1792]{1,0:T(8,128)(2,1)} %get-tuple-element.7.grad, bf16[256,1792]{1,0:T(8,128)(2,1)} %get-tuple-element.8.curv, bf16[256,1792]{1,0:T(8,128)(2,1)} %probe.1, f32[256,1792]{1,0:T(8,128)} %moment.1, ...), custom_call_target="tpu_custom_call" | custom-call | tf_op jit(solution)/shard_map/pallas_call | solution.py:582
